TPU v7x, 1024 devices: a whole 8x8x8 slice. The times are simulated.
1024 devices in a mesh: expert: 64 (over x_hi, z, core), context: 16 (over y, x_lo).
Axes of the slice: x: 8 (x_hi: 4, x_lo: 2; x = x_hi * 2 + x_lo), y: 8, z: 8, core: 2. Of those that a mesh axis runs over, the one named last changes fastest.
Arguments:
- queries: bfloat16 [64, 16, 4096], P('expert', None, 'context'), may hold values from -2.5 to 2.5
- keys_values: bfloat16 [64, 2048, 512], P('expert', 'context'), may hold values from -2.5 to 2.5
- out_proj: bfloat16 [4096, 4096], P('context'), may hold values from -0.09375 to 0.09375
- norm_gain: float32 [4096], P('context'), may hold values from 0.5 to 2
- expert_ids: int32 [64, 16, 8], P('expert'), may hold values from 0 to 63, all different within a row; in each aligned block of 16 rows (0 to 15, 16 to 31, ..., all dimensions but the last counted through in order) at most 3 rows name the same one
- route_logits: float32 [64, 16, 8], P('expert'), may hold values from -6 to 6
- home: int32 [64], replicated, may hold values from 0 to 63, each once
- gate_up: bfloat16 [64, 4096, 3072], P('expert', 'context'), may hold values from -0.09375 to 0.09375
- down: bfloat16 [64, 1536, 4096], P('expert', None, 'context'), may hold values from -0.15625 to 0.15625
Outputs:
- moe_out: bfloat16 [64, 16, 4096], P('expert', None, 'context')
Inputs may be any that keep to these rules, and one draw needn't show every extreme that they name: `expert_ids`: in each sequence's 16 rows no expert is named by more than 3 rows, a bound that some block reaches. `home`: each slot holds exactly one expert.
All inputs are finite; a program needn't handle non-finite values.
Results may differ from a plain program's by a relative error of at most 0.04.
Values may be sent and summed in bfloat16 or wider, within the bound.
A program may use at most 32 MiB of HBM per device.

v0:
```python
import jax
import jax.numpy as jnp
from jax import lax
from jax.sharding import PartitionSpec as P

D = 4096
FF = 1536
HQ = 32
HD = 128
KVH = 2
EXPERTS = 64
TOPK = 8
MROWS = 16
CAP = 3


def slot_tables(expert_row, home):
    slot = jnp.sum(
        (expert_row[:, :, None] == jnp.arange(EXPERTS, dtype=jnp.int32)).astype(jnp.int32)
        * home[None, None, :],
        axis=2,
    )
    flat = slot.reshape(-1)
    onehot = (flat[:, None] == jnp.arange(EXPERTS, dtype=jnp.int32)).astype(jnp.int32)
    before = jnp.cumsum(onehot, axis=0) - onehot
    rank = jnp.sum(before * onehot, axis=1)
    place = flat * CAP + rank
    table = place[:, None] == jnp.arange(EXPERTS * CAP, dtype=jnp.int32)
    return table.reshape(MROWS, TOPK, EXPERTS * CAP)


def attend_block(query, keys, values, query_pos):
    scores = jnp.einsum("ihd,td->iht", query, keys, preferred_element_type=jnp.float32) * HD ** (
        -0.5
    )
    key_pos = jnp.arange(keys.shape[0], dtype=jnp.int32)
    visible = key_pos[None, :] <= query_pos[:, None]
    weight = jnp.where(visible[:, None, :], jnp.exp(scores), 0.0)
    numer = jnp.einsum(
        "iht,td->ihd", weight.astype(jnp.bfloat16), values, preferred_element_type=jnp.float32
    )
    return (jnp.sum(weight, axis=2), numer)


def body(queries, keys_values, out_proj, norm_gain, expert_ids, route_logits, home, gate_up, down):
    contexts = lax.axis_size("context")
    position = lax.axis_index("context")
    per_dev = HQ // contexts
    group = HQ // KVH
    head = position * per_dev // group
    query = queries[0].reshape(MROWS, per_dev, HD)
    tok_rows = keys_values.shape[1]
    length = tok_rows * contexts
    query_pos = (jnp.arange(MROWS, dtype=jnp.int32) + 1) * (length // MROWS) - 1
    rows = lax.all_gather(keys_values, "context", axis=1, tiled=True)[0]
    keys = lax.dynamic_slice_in_dim(rows, head * HD, HD, 1)
    values = lax.dynamic_slice_in_dim(rows, (KVH + head) * HD, HD, 1)
    denom_add, numer_add = attend_block(query, keys, values, query_pos)
    attended = (numer_add / denom_add[..., None]).reshape(MROWS, per_dev * HD).astype(jnp.bfloat16)
    projected = (
        lax.psum_scatter(
            lax.dot_general(
                out_proj, attended, (((0,), (1,)), ((), ())), preferred_element_type=jnp.float32
            ).astype(jnp.bfloat16),
            "context",
            scatter_dimension=0,
            tiled=True,
        )
        .astype(jnp.float32)
        .T
    )
    normed_in = (projected * norm_gain).astype(jnp.bfloat16)
    squares = jnp.sum(projected * projected, axis=1).astype(jnp.bfloat16)
    tables = slot_tables(expert_ids[0], home)
    picks = jnp.sum(tables.astype(jnp.float32), axis=1).astype(jnp.bfloat16)
    dims = (((0,), (0,)), ((), ()))
    slot_rows = (
        lax.dot_general(picks, normed_in, dims, preferred_element_type=jnp.float32)
        .astype(jnp.bfloat16)
        .reshape(EXPERTS, CAP, -1)
    )
    slot_squares = (
        lax.dot_general(picks, squares[:, None], dims, preferred_element_type=jnp.float32)
        .astype(jnp.bfloat16)
        .reshape(EXPERTS, CAP)
    )
    rows = lax.all_to_all(slot_rows, "expert", split_axis=0, concat_axis=0, tiled=True)
    row_squares = lax.all_to_all(slot_squares, "expert", split_axis=0, concat_axis=0, tiled=True)
    count = rows.shape[1]
    local = gate_up.shape[0]
    sources = rows.shape[0] // local
    grouped = rows.reshape(sources, local, count, rows.shape[2])
    parts = jnp.einsum("sekd,edf->sekf", grouped, gate_up, preferred_element_type=jnp.float32)
    square_terms = row_squares.reshape(sources, local, count).astype(jnp.float32)
    halves = parts.reshape(sources, local, count, 2, FF)
    tiled = jnp.broadcast_to(square_terms[..., None], (sources, local, count, contexts))
    share = lax.psum_scatter(
        halves.astype(jnp.bfloat16), "context", scatter_dimension=4, tiled=True
    ).astype(jnp.float32)
    total_sq = lax.psum_scatter(
        tiled.astype(jnp.bfloat16), "context", scatter_dimension=3, tiled=True
    ).astype(jnp.float32)
    scale = lax.rsqrt(total_sq[..., 0] / D + 1e-06)[..., None]
    hidden_share = (jax.nn.silu(scale * share[..., 0, :]) * (scale * share[..., 1, :])).astype(
        jnp.bfloat16
    )
    hidden_act = lax.all_gather(hidden_share, "context", axis=3, tiled=True)
    result = jnp.einsum(
        "sekf,efd->sekd", hidden_act, down, preferred_element_type=jnp.float32
    ).astype(jnp.bfloat16)
    returned = lax.all_to_all(
        result.reshape(rows.shape[0], count, result.shape[3]),
        "expert",
        split_axis=0,
        concat_axis=0,
        tiled=True,
    )
    raised = jnp.exp(route_logits[0])
    route_low = (raised / jnp.sum(raised, axis=1, keepdims=True)).astype(jnp.bfloat16)
    combine = jnp.sum(
        tables.astype(jnp.float32) * route_low.astype(jnp.float32)[:, :, None], axis=1
    ).astype(jnp.bfloat16)
    moe_out = jnp.dot(
        combine, returned.reshape(EXPERTS * CAP, -1), preferred_element_type=jnp.float32
    ).astype(jnp.bfloat16)
    return moe_out[None]


def solution(mesh):
    in_specs = (
        P("expert", None, "context"),
        P("expert", "context", None),
        P("context", None),
        P("context"),
        P("expert", None, None),
        P("expert", None, None),
        P(),
        P("expert", "context", None),
        P("expert", None, "context"),
    )
    out_specs = P("expert", None, "context")
    return jax.shard_map(body, mesh=mesh, in_specs=in_specs, out_specs=out_specs, check_vma=False)
```

profile of v0, /device:TPU:1, one launch (start us, length us, event | category | flops | bytes accessed | tf_op | source)
XLA Modules:
  0.0 386.8 jit_solution(3297262326864806914)
XLA Ops:
  6.5 0.0 copy-start
  6.5 0.0 all-gather.2.cloned.1.call-start
  6.5 0.7 all-gather.2.cloned.1.call-update
  7.3 0.0 reduce-scatter.6.cloned.1.call-start
  7.3 0.7 exponential_reduce_fusion
  8.0 0.7 fusion.34
  8.7 0.1 copy.46
  8.8 0.7 reshape_squeeze.3
  9.5 0.8 copy.45
  10.3 1.1 select_reduce_fusion.2
  11.3 0.1 eq.48
  11.4 0.0 copy-start.3
  11.4 0.1 fusion.21
  11.5 0.2 reduce_window_sum.11
  11.7 0.2 select_reduce_fusion.1
  11.9 0.1 reduce_sum.67
  12.0 0.1 iota_compare_fusion
  12.1 81.1 %all-gather.2.cloned.1.call-done = bf16[1,2048,512]{2,1,0:T(8,128)(2,1)} async-done(((bf16[1,128,512]{2,1,0:T(8,128)(2,1)}), bf16[1,2048,512]{2,1,0:T(8,128)(2,1)}) %all-gather.2.cloned.1.call-update) | async-done | bytes 2097168 | tf_op jit(solution)/shard_map/all_gather | solution.py:55
  93.2 1.4 fusion.39
  94.6 1.3 fusion.8
  95.9 0.0 copy-done
  95.9 1.0 fusion
  96.9 0.0 reduce-scatter.6.cloned.1.call-update
  96.9 0.0 reduce-scatter.8.cloned.1.call-start
  97.0 0.2 select_reduce_fusion
  97.2 73.4 %reduce-scatter.6.cloned.1.call-done = bf16[256,16]{0,1:T(8,128)(2,1)} async-done(((bf16[4096,16]{0,1:T(8,128)(2,1)}), bf16[256,16]{0,1:T(8,128)(2,1)}) %reduce-scatter.6.cloned.1.call-update) | async-done | bytes 8208 | tf_op jit(solution)/shard_map/reduce_scatter | solution.py:61
  170.6 0.0 copy-done.3
  170.6 0.9 convolution_convert_fusion.3
  171.5 0.1 reshape.186
  171.5 37.4 %all_to_all.20 = bf16[64,3,256]{2,1,0:T(4,128)(2,1)S(1)} all-to-all(bf16[64,3,256]{2,1,0:T(4,128)(2,1)S(1)} %reshape.186), channel_id=1, replica_groups=mesh['expert'=64,'context'=16] {'expert'}, dimensions={0} | all-to-all | bytes 196608 | tf_op jit(solution)/shard_map/all_to_all | solution.py:87
  209.0 1.9 fusion.1
  210.9 1.7 convert_element_type.142
  212.6 8.7 %copy.58 = bf16[64,1,3,2,1536]{0,2,3,1,4:T(4,128)(2,1)} copy(bf16[64,1,3,2,1536]{4,3,0,2,1:T(2,128)(2,1)} %convert_element_type.142) | data formatting | bytes 2359296
  221.3 0.0 copy-start.2
  221.3 6.6 %reshape.199 = bf16[1536,384]{1,0:T(8,128)(2,1)} reshape(bf16[1536,1,2,3,64]{4,3,2,1,0:T(4,128)(2,1)} %bitcast.86) | data formatting | bytes 2359296
  227.9 0.0 reduce-scatter.8.cloned.1.call-update
  227.9 0.0 copy-done.2
  227.9 0.1 fusion.22
  228.0 0.1 fusion.32
  228.1 0.8 all_to_all.16
  228.9 4.4 %all-to-all-start = ((bf16[64,1,3]{2,1,0:T(2,128)(2,1)}), bf16[64,1,3]{2,1,0:T(2,128)(2,1)S(1)}, u32[]{:S(2)}, u32[]{:S(2)}) async-start(bf16[64,1,3]{2,1,0:T(2,128)(2,1)} %all_to_all.16), calls=%async_computation.1 | async-start | bytes 65536 | tf_op jit(solution)/shard_map/all_to_all | solution.py:88
  233.3 1.3 dynamic-slice.2
  234.6 10.6 %all-to-all-done = bf16[64,1,3]{2,1,0:T(2,128)(2,1)S(1)} async-done(((bf16[64,1,3]{2,1,0:T(2,128)(2,1)}), bf16[64,1,3]{2,1,0:T(2,128)(2,1)S(1)}, u32[]{:S(2)}, u32[]{:S(2)}) %all-to-all-start) | async-done | bytes 416 | tf_op jit(solution)/shard_map/all_to_all | solution.py:88
  245.2 0.1 copy.50
  245.3 50.2 %all-reduce = bf16[64,1,3,16]{0,2,3,1:T(4,128)(2,1)S(1)} all-reduce(bf16[64,1,3,16]{0,2,3,1:T(4,128)(2,1)S(1)} %broadcast_in_dim.18), channel_id=3, replica_groups=mesh['expert'=64,'context'=16] {'context'}, use_global_device_ids=true, to_apply=%region_9.10.clone | all-reduce | flops 3072 | bytes 12288
  295.4 0.7 rsqrt_bitcast_fusion
  296.1 0.0 reduce-scatter.8.cloned.1.call-done
  296.1 1.0 reshape.200
  297.2 0.2 copy.59
  297.3 0.0 copy-start.1
  297.4 0.1 fusion.18
  297.5 0.1 copy.53
  297.6 40.5 %all_gather.7 = bf16[64,1,3,1536]{0,2,1,3:T(4,128)(2,1)} all-gather(bf16[64,1,3,96]{0,2,1,3:T(4,128)(2,1)S(1)} %copy.53), channel_id=1, replica_groups=mesh['expert'=64,'context'=16] {'context'}, dimensions={3}, use_global_device_ids=true | all-gather | bytes 626688 | tf_op jit(solution)/shard_map/all_gather | solution.py:107
  338.1 2.5 copy.54
  340.7 0.0 copy-done.1
  340.7 0.3 convolution_convert_fusion.2
  341.0 0.1 copy.55
  341.1 38.3 %all_to_all.21 = bf16[64,3,256]{2,1,0:T(4,128)(2,1)S(1)} all-to-all(bf16[64,3,256]{2,1,0:T(4,128)(2,1)S(1)} %copy.55), channel_id=1, replica_groups=mesh['expert'=64,'context'=16] {'expert'}, dimensions={0} | all-to-all | bytes 196608 | tf_op jit(solution)/shard_map/all_to_all | solution.py:111
  379.5 0.1 reshape.190
  379.6 0.7 fusion.7
  (5 shorter events, 0.1 us)
Async XLA Ops:
  6.5 89.3 %copy-start = (bf16[256,4096]{1,0:T(8,128)(2,1)S(1)}, bf16[256,4096]{1,0:T(8,128)(2,1)}, u32[]{:S(2)}) copy-start(bf16[256,4096]{1,0:T(8,128)(2,1)} %param.11) | copy-start | bytes 6291460
  6.5 86.7 %all-gather.2.cloned.1.call-start = ((), (), s32[]{:S(2)}) async-start(), calls=%async_computation.5 | async-start | bytes 2228224 | tf_op jit(solution)/shard_map/all_gather | solution.py:55
  7.3 163.3 %reduce-scatter.6.cloned.1.call-start = ((), (), s32[]{:S(2)}) async-start(), calls=%async_computation.6 | async-start | bytes 139264 | tf_op jit(solution)/shard_map/reduce_scatter | solution.py:61
  11.4 159.1 %copy-start.3 = (f32[256]{0:T(256)S(1)}, f32[256]{0:T(256)}, u32[]{:S(2)}) copy-start(f32[256]{0:T(256)} %param.12) | copy-start | bytes 3076
  96.9 199.2 %reduce-scatter.8.cloned.1.call-start = ((), (), s32[]{:S(2)}) async-start(), calls=%async_computation.7 | async-start | bytes 1253376
  221.3 6.6 %copy-start.2 = (bf16[256,16]{0,1:T(8,128)(2,1)S(1)}, bf16[256,16]{0,1:T(8,128)(2,1)}, u32[]{:S(2)}) copy-start(bf16[256,16]{0,1:T(8,128)(2,1)} %reduce-scatter.6.cloned.1.call-done) | copy-start | bytes 24580
  228.9 16.2 %all-to-all-start = ((bf16[64,1,3]{2,1,0:T(2,128)(2,1)}), bf16[64,1,3]{2,1,0:T(2,128)(2,1)S(1)}, u32[]{:S(2)}, u32[]{:S(2)}) async-start(bf16[64,1,3]{2,1,0:T(2,128)(2,1)} %all_to_all.16), calls=%async_computation.1 | async-start | bytes 65536 | tf_op jit(solution)/shard_map/all_to_all | solution.py:88
  297.3 43.3 %copy-start.1 = (bf16[1,1536,256]{2,1,0:T(8,128)(2,1)S(1)}, bf16[1,1536,256]{2,1,0:T(8,128)(2,1)}, u32[]{:S(2)}) copy-start(bf16[1,1536,256]{2,1,0:T(8,128)(2,1)} %param.17) | copy-start | bytes 2359300
Sparse Core Ops, SparseCore 0:
  10.0 83.1 all-gather.1
  97.1 73.4 reduce-scatter.5
  228.0 58.9 reduce-scatter.7
where the time goes:
time: 388 us; the launch traced here: 387 us
  waiting for transfers between devices  166 us (43%)
  blocking collectives  166 us (43%)
  local copies, waits for them, and re-layouts  25 us (6%)
  between operations  13.3 us (3%)
  matrix products  7.66 us (2%)
  starting transfers between devices  4.45 us (1%)
  other arithmetic  4.07 us (1%)
    all_gather x1, waiting for transfers between devices, body(): rows = lax.all_gather(keys_values, 'context', axis=1, tiled=True)[0]  81.1 us
    reduce_scatter x1, waiting for transfers between devices, body(): lax.psum_scatter(lax.dot_general(out_proj, attended, (((0,), (1,)), ((),...  73.4 us
    unnamed x1, blocking collectives  50.2 us
    all_gather x1, blocking collectives, body(): hidden_act = lax.all_gather(hidden_share, 'context', axis=3, tiled=True)  40.5 us
    all_to_all x1, blocking collectives, body(): lax.all_to_all(result.reshape(rows.shape[0], count, result.shape[3]), 'ex...  38.3 us
    all_to_all x1, blocking collectives, body(): lax.all_to_all(slot_rows, 'expert', split_axis=0, concat_axis=0, tiled=True)  37.4 us
    unnamed x13, local copies, waits for them, and re-layouts  17.8 us
    all_to_all x1, waiting for transfers between devices, body(): lax.all_to_all(slot_squares, 'expert', split_axis=0, concat_axis=0, tiled...  10.6 us
  transfers between devices with their start and end apart: 4, of which 3 were waited for; matrix products, arithmetic and copies ran while one was open for 2% of the time, Pallas kernels for 0%

commit v1 on v0

v1 whole, which is shorter than its diff:
```python
import functools

import jax
import jax.numpy as jnp
from jax import lax
from jax.experimental import pallas as pl
from jax.experimental.pallas import tpu as pltpu
from jax.sharding import PartitionSpec as P

MESH = pl.DeviceIdType.MESH
BF = jnp.bfloat16
F32 = jnp.float32

D = 4096
FF = 1536
HD = 128
MROWS = 16
TOPK = 8
CTX = 16
NY = 8
NZ = 8
NXC = 8
SLOTS = 256
ROWS = 192
RB = 48
CB = 384
CHUNK = 6 * RB + 16
SEND_ORDER = [(dy, dx) for dy in (4, 3, 5, 2, 6, 1, 7, 0) for dx in (1, 0) if (dy, dx) != (0, 0)]


def iota(shape, dim):
    return lax.broadcasted_iota(jnp.int32, shape, dim)


def dot(a, b, ca=1, cb=0):
    return lax.dot_general(a, b, (((ca,), (cb,)), ((), ())), preferred_element_type=F32)


def kernel(
    q_ref, kv_hbm, op_hbm, gain_ref, ids_ref, logits_ref, home_ref, gu_hbm, dn_hbm, out_ref,
    kv, op, gu, dn, qall, nb, nr, cs, cr, d1s, d1r, d2s, d2r, es, er, acc, fs, hid, g1s, g1r, g2s, g2r,
    picks_ref, combine_ref, perm_ref,
    load_sem, send_sem, q_sem, n_sem, c_sem, d1_sem, d2_sem, e_sem, fsend_sem, f_sem, g1_sem, g2_sem,
):
    e = lax.axis_index("expert")
    c = lax.axis_index("context")
    y, xl = c // 2, c % 2
    core, z, xh = e % 2, (e // 2) % NZ, e // (2 * NZ)
    xc = xh * 2 + core

    loads = [
        pltpu.make_async_copy(src, dst, load_sem.at[i])
        for i, (src, dst) in enumerate([(kv_hbm.at[0], kv), (op_hbm, op), (gu_hbm.at[0], gu), (dn_hbm.at[0], dn)])
    ]
    for load in loads:
        load.start()

    def ctx_peer(dy, dx):
        return ((y + dy) % NY) * 2 + (xl + dx) % 2

    def z_peer(d):
        other = (z + d) % NZ
        return other, (xh * NZ + other) * 2 + core

    def xc_peer(d):
        other = (xc + d) % NXC
        return other, ((other // 2) * NZ + z) * 2 + other % 2

    barrier = pltpu.get_barrier_semaphore()

    def greet(ee, cc):
        pl.semaphore_signal(barrier, inc=1, device_id=(ee, cc), device_id_type=MESH)

    for dy, dx in SEND_ORDER:
        greet(e, ctx_peer(dy, dx))
    for d in range(1, 8):
        greet(z_peer(d)[1], c)
        greet(xc_peer(d)[1], c)

    ids = ids_ref[0]
    logits = logits_ref[0]
    raised = jnp.exp(logits)
    route = (raised / jnp.sum(raised, axis=1, keepdims=True)).astype(BF).astype(F32)
    lanes = iota((MROWS, 64), 1)
    chosen = jnp.zeros((MROWS, 64), F32)
    weights = jnp.zeros((MROWS, 64), F32)
    for j in range(TOPK):
        hit = ids[:, j : j + 1] == lanes
        chosen = chosen + jnp.where(hit, 1.0, 0.0)
        weights = weights + jnp.where(hit, route[:, j : j + 1], 0.0)
    r = iota((SLOTS, 64), 0)
    r_xc = (r >> 2) & 7
    r_slot = ((r_xc >> 1) * NZ + (r >> 5)) * 2 + (r_xc & 1)
    lands = jnp.where(home_ref[...] == r_slot, 1.0, 0.0).astype(BF)
    chosen_r = dot(chosen.astype(BF), lands, 1, 1)
    weights_r = dot(weights.astype(BF), lands, 1, 1)
    earlier = jnp.where(iota((MROWS, MROWS), 1) < iota((MROWS, MROWS), 0), 1.0, 0.0).astype(BF)
    rank = dot(earlier, chosen_r.astype(BF))
    right_rank = rank == (iota((MROWS, SLOTS), 1) & 3).astype(F32)
    picks_ref[...] = jnp.where(right_rank, chosen_r, 0.0).astype(BF)
    combine_ref[...] = jnp.where(right_rank, weights_r, 0.0).astype(BF)
    pr, pc = iota((SLOTS, SLOTS), 0), iota((SLOTS, SLOTS), 1)
    perm_ref[...] = jnp.where(pc == ((pr >> 2) & 7) * 32 + (pr >> 5) * 4 + (pr & 3), 1.0, 0.0).astype(BF)

    qall[c] = q_ref[0]
    pl.semaphore_wait(barrier, 29)

    def send(src, dst, s_sem, r_sem, ee, cc):
        pltpu.make_async_remote_copy(
            src_ref=src, dst_ref=dst, send_sem=s_sem, recv_sem=r_sem, device_id=(ee, cc), device_id_type=MESH
        ).start()

    def await_bytes(ref, sem):
        pltpu.make_async_copy(ref, ref, sem).wait()

    for dy, dx in SEND_ORDER:
        send(q_ref.at[0], qall.at[c], send_sem.at[0], q_sem, e, ctx_peer(dy, dx))
    loads[0].wait()
    await_bytes(qall.at[pl.ds(0, 15)], q_sem)

    visible = (iota((128, 128), 0) & 15) >= c
    for g in range(2):
        key, value = kv[:, g * HD : (g + 1) * HD], kv[:, (2 + g) * HD : (3 + g) * HD]
        denoms = []
        for p in range(2):
            query = qall[8 * g : 8 * g + 8, :, p * HD : (p + 1) * HD].reshape(128, HD)
            scores = dot(query, key, 1, 1) * HD ** (-0.5)
            weight = jnp.where(visible, jnp.exp(scores), 0.0)
            denoms.append(jnp.sum(weight, axis=1, keepdims=True))
            numer = dot(weight.astype(BF), value)
            nb[8 * g : 8 * g + 8, :, p * HD : (p + 1) * HD] = numer.astype(BF).reshape(8, MROWS, HD)
        lane = iota((128, 128), 1)
        both = jnp.where(lane < 64, denoms[0], denoms[1])
        high = both.astype(BF).astype(F32)
        packed = jnp.where((lane & 63) < 32, high, both - high)
        nb[8 * g : 8 * g + 8, :, 256:384] = packed.astype(BF).reshape(8, MROWS, 128)

    for dy, dx in SEND_ORDER:
        peer = ctx_peer(dy, dx)
        send(nb.at[peer], nr.at[dy * 2 + dx], send_sem.at[1], n_sem, e, peer)
    nr[0] = nb[c]
    await_bytes(nr.at[pl.ds(1, 15)], n_sem)
    total = nr[0].astype(F32)
    for j in range(1, CTX):
        total = total + nr[j].astype(F32)
    denom0 = total[:, 256:257] + total[:, 288:289]
    denom1 = total[:, 320:321] + total[:, 352:353]
    attended = jnp.concatenate([total[:, 0:128] / denom0, total[:, 128:256] / denom1], axis=1).astype(BF)

    loads[1].wait()
    for dy, dx in SEND_ORDER + [(0, 0)]:
        peer = ctx_peer(dy, dx)
        j = dy * 2 + dx
        part = dot(attended, op[:, pl.ds(pl.multiple_of(peer * 256, 256), 256)]).astype(BF)
        if j == 0:
            cr[0] = part
        else:
            cs[j] = part
            send(cs.at[j], cr.at[j], send_sem.at[2], c_sem, e, peer)
    await_bytes(cr.at[pl.ds(1, 15)], c_sem)
    projected = cr[0].astype(F32)
    for j in range(1, CTX):
        projected = projected + cr[j].astype(F32)
    gain = gain_ref[...]
    normed = (projected * gain).astype(BF)

    d1s[...] = dot(picks_ref[...], normed, 0, 0).astype(BF).reshape(NZ, 32, 256)
    for d in (4, 3, 5, 2, 6, 1, 7):
        other, peer = z_peer(d)
        send(d1s.at[other], d1r.at[z], send_sem.at[3], d1_sem, peer, c)
    d1r[z] = d1s[z]
    await_bytes(d1r.at[pl.ds(0, 7)], d1_sem)
    d2s[...] = dot(perm_ref[...], d1r[...].reshape(SLOTS, 256)).astype(BF).reshape(NXC, 32, 256)
    for d in (4, 3, 5, 2, 6, 1, 7):
        other, peer = xc_peer(d)
        send(d2s.at[other], d2r.at[xc], send_sem.at[4], d2_sem, peer, c)
    d2r[xc] = d2s[xc]
    squeeze = jnp.where(
        iota((ROWS, SLOTS), 1) == (iota((ROWS, SLOTS), 0) & 63) * 4 + (iota((ROWS, SLOTS), 0) >> 6), 1.0, 0.0
    ).astype(BF)
    await_bytes(d2r.at[pl.ds(0, 7)], d2_sem)
    rows32 = dot(squeeze, d2r[...].reshape(SLOTS, 256))
    rows = rows32.astype(BF)

    raw = rows32 * (1.0 / gain)
    squares = jnp.sum(raw * raw, axis=1, keepdims=True)
    lane16 = iota((16, 128), 1)
    tiles = []
    for rb in range(4):
        a, b, cc = (squares[rb * RB + t * 16 : rb * RB + t * 16 + 16] for t in range(3))
        tiles.append(jnp.where(lane16 < 32, a, jnp.where(lane16 < 64, b, cc)).astype(BF))
    loads[2].wait()
    my_cb = c // 4
    for step in (2, 1, 3, 0):
        cb = (my_cb + step) % 4
        for half in range(2):
            start = pl.multiple_of(half * FF + cb * CB, 128)
            part = dot(rows, gu[:, pl.ds(start, CB)]).astype(BF)
            for rb in range(4):
                for t in range(3):
                    at = (half * 3 + t) * RB
                    es[cb * 4 + rb, at : at + RB, :] = part[rb * RB : rb * RB + RB, t * 128 : t * 128 + 128]
        for rb in range(4):
            es[cb * 4 + rb, 6 * RB : CHUNK, :] = tiles[rb]
        for rb in range(4):
            peer = cb * 4 + rb
            slot = ((peer // 2 - y) % NY) * 2 + (peer + xl) % 2

            @pl.when(peer != c)
            def _():
                send(es.at[peer], er.at[slot], send_sem.at[5], e_sem.at[slot], e, peer)

    acc[...] = es[c].astype(F32)
    for n, (dy, dx) in enumerate(SEND_ORDER):
        j = dy * 2 + dx
        await_bytes(er.at[j], e_sem.at[j])
        acc[...] += er[j].astype(F32)
    scale16 = lax.rsqrt(acc[6 * RB : CHUNK, :] * (1.0 / D) + 1e-06)
    scale = jnp.concatenate([scale16[:, 0:1], scale16[:, 32:33], scale16[:, 64:65]], axis=0)
    for t in range(3):
        gate = acc[t * RB : t * RB + RB, :] * scale
        upper = acc[(3 + t) * RB : (4 + t) * RB, :] * scale
        fs[:, t * 128 : t * 128 + 128] = (gate / (1.0 + jnp.exp(-gate)) * upper).astype(BF)
    row_at = pl.multiple_of((c % 4) * RB, 16)
    col_at = pl.multiple_of(my_cb * CB, 128)
    mine = hid.at[pl.ds(row_at, RB), pl.ds(col_at, CB)]
    for dy, dx in SEND_ORDER:
        send(fs, mine, fsend_sem.at[dy * 2 + dx], f_sem.at[dy * 2 + dx], e, ctx_peer(dy, dx))
    hid[pl.ds(row_at, RB), pl.ds(col_at, CB)] = fs[...]
    stretch = jnp.where(
        iota((SLOTS, ROWS), 0) == (iota((SLOTS, ROWS), 1) & 63) * 4 + (iota((SLOTS, ROWS), 1) >> 6), 1.0, 0.0
    ).astype(BF)
    loads[3].wait()
    for dy, dx in SEND_ORDER:
        await_bytes(fs, f_sem.at[dy * 2 + dx])
    result = dot(hid[...], dn[...]).astype(BF)

    g1s[...] = dot(stretch, result).astype(BF).reshape(NXC, 32, 256)
    for d in (4, 3, 5, 2, 6, 1, 7):
        other, peer = xc_peer(d)
        send(g1s.at[other], g1r.at[xc], send_sem.at[7], g1_sem, peer, c)
    g1r[xc] = g1s[xc]
    await_bytes(g1r.at[pl.ds(0, 7)], g1_sem)
    g2s[...] = dot(perm_ref[...], g1r[...].reshape(SLOTS, 256)).astype(BF).reshape(NZ, 32, 256)
    for d in (4, 3, 5, 2, 6, 1, 7):
        other, peer = z_peer(d)
        send(g2s.at[other], g2r.at[z], send_sem.at[8], g2_sem, peer, c)
    g2r[z] = g2s[z]
    await_bytes(g2r.at[pl.ds(0, 7)], g2_sem)
    out_ref[0] = dot(combine_ref[...], g2r[...].reshape(SLOTS, 256)).astype(BF)

    await_bytes(qall.at[pl.ds(0, 15)], send_sem.at[0])
    await_bytes(nr.at[pl.ds(0, 15)], send_sem.at[1])
    await_bytes(cr.at[pl.ds(0, 15)], send_sem.at[2])
    await_bytes(d1r.at[pl.ds(0, 7)], send_sem.at[3])
    await_bytes(d2r.at[pl.ds(0, 7)], send_sem.at[4])
    await_bytes(er.at[pl.ds(0, 15)], send_sem.at[5])
    for j in range(1, CTX):
        await_bytes(fs, fsend_sem.at[j])
    await_bytes(g1r.at[pl.ds(0, 7)], send_sem.at[7])
    await_bytes(g2r.at[pl.ds(0, 7)], send_sem.at[8])


def body(queries, keys_values, out_proj, norm_gain, expert_ids, route_logits, home, gate_up, down):
    vm = pl.BlockSpec(memory_space=pltpu.VMEM)
    hb = pl.BlockSpec(memory_space=pl.ANY)
    dma = pltpu.SemaphoreType.DMA
    vmem = pltpu.VMEM
    return pl.pallas_call(
        kernel,
        out_shape=jax.ShapeDtypeStruct((1, MROWS, 256), BF),
        in_specs=[vm, hb, hb, vm, vm, vm, vm, hb, hb],
        out_specs=vm,
        scratch_shapes=[
            vmem((128, 512), BF),
            vmem((256, D), BF),
            vmem((256, 2 * FF), BF),
            vmem((FF, 256), BF),
            vmem((CTX, MROWS, 256), BF),
            vmem((CTX, MROWS, 384), BF),
            vmem((CTX, MROWS, 384), BF),
            vmem((CTX, MROWS, 256), BF),
            vmem((CTX, MROWS, 256), BF),
            vmem((NZ, 32, 256), BF),
            vmem((NZ, 32, 256), BF),
            vmem((NXC, 32, 256), BF),
            vmem((NXC, 32, 256), BF),
            vmem((CTX, CHUNK, 128), BF),
            vmem((CTX, CHUNK, 128), BF),
            vmem((CHUNK, 128), F32),
            vmem((RB, CB), BF),
            vmem((ROWS, FF), BF),
            vmem((NXC, 32, 256), BF),
            vmem((NXC, 32, 256), BF),
            vmem((NZ, 32, 256), BF),
            vmem((NZ, 32, 256), BF),
            vmem((MROWS, SLOTS), BF),
            vmem((MROWS, SLOTS), BF),
            vmem((SLOTS, SLOTS), BF),
            dma((4,)),
            dma((9,)),
            dma, dma, dma, dma, dma,
            dma((CTX,)),
            dma((CTX,)),
            dma((CTX,)),
            dma, dma,
        ],
        compiler_params=pltpu.CompilerParams(
            collective_id=0, has_side_effects=True, vmem_limit_bytes=40 * 1024 * 1024
        ),
    )(
        queries, keys_values, out_proj, norm_gain.reshape(1, 256), expert_ids, route_logits,
        home.reshape(1, 64), gate_up, down,
    )


def solution(mesh):
    in_specs = (
        P("expert", None, "context"),
        P("expert", "context", None),
        P("context", None),
        P("context"),
        P("expert", None, None),
        P("expert", None, None),
        P(),
        P("expert", "context", None),
        P("expert", None, "context"),
    )
    out_specs = P("expert", None, "context")
    return jax.shard_map(body, mesh=mesh, in_specs=in_specs, out_specs=out_specs, check_vma=False)
```

time: 388 us -> 127 us (0.33)
  blocking collectives: 166 us -> 0 us
  waiting for transfers between devices: 166 us -> 0 us
  Pallas kernels: 0 us -> 118 us
  local copies, waits for them, and re-layouts: 25 us -> 9.18 us
  between operations: 13.3 us -> 0.02 us
  matrix products: 7.66 us -> 0 us
  starting transfers between devices: 4.45 us -> 0 us
  other arithmetic: 4.07 us -> 0 us
    pallas_call x0 -> x1, Pallas kernels: none -> 118 us  [body(): pl.pallas_call(kernel, out_shape=jax.ShapeDtypeStruct((1, MROWS, 256), BF...]
    all_gather x1 -> x0, waiting for transfers between devices: 81.1 us -> none  [body(): rows = lax.all_gather(keys_values, 'context', axis=1, tiled=True)[0]]
    all_to_all x2 -> x0, blocking collectives: 75.8 us -> none  [the longest x1 38.3 us: body(): lax.all_to_all(result.reshape(rows.shape[0], count, result.shape[3]), 'ex...]
    reduce_scatter x1 -> x0, waiting for transfers between devices: 73.4 us -> none  [body(): lax.psum_scatter(lax.dot_general(out_proj, attended, (((0,), (1,)), ((),...]
    unnamed x1 -> x0, blocking collectives: 50.2 us -> none
    all_gather x1 -> x0, blocking collectives: 40.5 us -> none  [body(): hidden_act = lax.all_gather(hidden_share, 'context', axis=3, tiled=True)]
    all_to_all x1 -> x0, waiting for transfers between devices: 10.6 us -> none  [body(): lax.all_to_all(slot_squares, 'expert', split_axis=0, concat_axis=0, tiled...]
    unnamed x13 -> x17, local copies, waits for them, and re-layouts: 17.8 us -> 9.18 us
  transfers between devices with their start and end apart: 4 -> 0, of which waited for: 3 -> 0; matrix products, arithmetic and copies ran while one was open for 2% -> 0% of each run, Pallas kernels for 0% -> 0%
where the time goes in v1:
time: 127 us
  Pallas kernels  118 us (93%)
  local copies, waits for them, and re-layouts  9.18 us (7%)
    pallas_call x1, Pallas kernels, body(): pl.pallas_call(kernel, out_shape=jax.ShapeDtypeStruct((1, MROWS, 256), BF...  118 us
    unnamed x17, local copies, waits for them, and re-layouts  9.18 us

profile of v1, /device:TPU:1, one launch (start us, length us, event | category | flops | bytes accessed | tf_op | source)
XLA Modules:
  0.0 126.7 jit_solution(2783631308435859372)
XLA Ops:
  0.0 0.8 copy.10.ids_ref
  0.8 0.8 copy.11.logits_ref
  1.5 0.0 copy-start
  1.5 1.6 %copy-done = bf16[256,4096]{1,0:T(8,128)(2,1)S(1)} copy-done((bf16[256,4096]{1,0:T(8,128)(2,1)S(1)}, bf16[256,4096]{1,0:T(8,128)(2,1)}, u32[]{:S(2)}) %copy-start) | copy-done | bytes 2097176
  3.1 0.0 copy-start.1
  3.1 1.4 %copy-done.1 = bf16[1,256,3072]{2,1,0:T(8,128)(2,1)S(1)} copy-done((bf16[1,256,3072]{2,1,0:T(8,128)(2,1)S(1)}, bf16[1,256,3072]{2,1,0:T(8,128)(2,1)}, u32[]{:S(2)}) %copy-start.1) | copy-done | bytes 1572888
  4.5 0.0 copy-start.2
  4.5 1.1 copy-done.2
  5.6 0.0 copy-start.3
  5.7 0.9 copy-done.3
  6.6 0.0 copy-start.4
  6.6 0.7 copy-done.4
  7.3 0.0 copy-start.5
  7.3 0.7 copy-done.5
  7.9 0.0 copy-start.6
  7.9 0.7 copy-done.6
  8.6 117.5 %shard_map.91 = bf16[1,16,256]{2,1,0:T(8,128)(2,1)S(1)} custom-call(bf16[1,16,256]{2,1,0:T(8,128)(2,1)S(1)} %copy-done.4, bf16[1,128,512]{2,1,0:T(8,128)(2,1)S(1)} %copy-done.3, bf16[256,4096]{1,0:T(8,128)(2,1)S(1)} %copy-done, f32[1,256]{1,0:T(1,128)S(1)} %bitcast.2, s32[1,16,8]{2,1,0:T(8,128)S(1)} %copy.10.ids_ref, f32[1,16,8]{2,1,0:T(8,128)S(1)} %copy.11.logits_ref, ...), custom_call_target="tpu_custom_call" | custom-call | tf_op jit(solution)/shard_map/pallas_call | solution.py:269
  126.1 0.6 copy.13
Async XLA Ops:
  1.5 1.6 %copy-start = (bf16[256,4096]{1,0:T(8,128)(2,1)S(1)}, bf16[256,4096]{1,0:T(8,128)(2,1)}, u32[]{:S(2)}) copy-start(bf16[256,4096]{1,0:T(8,128)(2,1)} %op_hbm.1) | copy-start | bytes 6291460
  3.1 1.4 %copy-start.1 = (bf16[1,256,3072]{2,1,0:T(8,128)(2,1)S(1)}, bf16[1,256,3072]{2,1,0:T(8,128)(2,1)}, u32[]{:S(2)}) copy-start(bf16[1,256,3072]{2,1,0:T(8,128)(2,1)} %gu_hbm.1) | copy-start | bytes 4718596
  4.5 1.1 copy-start.2
  5.6 0.9 copy-start.3
  6.6 0.7 copy-start.4
  7.3 0.7 copy-start.5
  7.9 0.7 copy-start.6

commit v2 on v1

--- a/solution.py
+++ b/solution.py
@@ -37,10 +37,11 @@
 
 
 def kernel(
-    q_ref, kv_hbm, op_hbm, gain_ref, ids_ref, logits_ref, home_ref, gu_hbm, dn_hbm, out_ref,
-    kv, op, gu, dn, qall, nb, nr, cs, cr, d1s, d1r, d2s, d2r, es, er, acc, fs, hid, g1s, g1r, g2s, g2r,
-    picks_ref, combine_ref, perm_ref,
-    load_sem, send_sem, q_sem, n_sem, c_sem, d1_sem, d2_sem, e_sem, fsend_sem, f_sem, g1_sem, g2_sem,
+    q_hbm, kv_hbm, op_hbm, gain_hbm, ids_hbm, logits_hbm, home_hbm, gu_hbm, dn_hbm, out_ref,
+    ids_ref, logits_ref, home_ref, gain_ref,
+    kv, op, gu, dn, qall, nb, nr, cs, cr, d1s, d1r, d2s, d2r, rows_ref, tiles_ref, own, xs, xr, ys, yr, acc, fs, hid,
+    g1s, g1r, g2s, g2r, picks_ref, combine_ref, perm_ref,
+    load_sem, send_sem, q_sem, n_sem, c_sem, d1_sem, d2_sem, x_sem, y_sem, fsend_sem, fy_sem, fx_sem, g1_sem, g2_sem,
 ):
     e = lax.axis_index("expert")
     c = lax.axis_index("context")
@@ -50,10 +51,16 @@
 
     loads = [
         pltpu.make_async_copy(src, dst, load_sem.at[i])
-        for i, (src, dst) in enumerate([(kv_hbm.at[0], kv), (op_hbm, op), (gu_hbm.at[0], gu), (dn_hbm.at[0], dn)])
+        for i, (src, dst) in enumerate(
+            [
+                (kv_hbm.at[0], kv), (op_hbm, op), (gu_hbm.at[0], gu), (dn_hbm.at[0], dn),
+                (q_hbm.at[0], qall.at[c]), (ids_hbm.at[0], ids_ref), (logits_hbm.at[0], logits_ref),
+                (home_hbm, home_ref), (gain_hbm, gain_ref),
+            ]
+        )
     ]
-    for load in loads:
-        load.start()
+    for i in (5, 6, 7, 4, 8, 0, 1, 2, 3):
+        loads[i].start()
 
     def ctx_peer(dy, dx):
         return ((y + dy) % NY) * 2 + (xl + dx) % 2
@@ -77,23 +84,24 @@
         greet(z_peer(d)[1], c)
         greet(xc_peer(d)[1], c)
 
-    ids = ids_ref[0]
-    logits = logits_ref[0]
-    raised = jnp.exp(logits)
-    route = (raised / jnp.sum(raised, axis=1, keepdims=True)).astype(BF).astype(F32)
-    lanes = iota((MROWS, 64), 1)
-    chosen = jnp.zeros((MROWS, 64), F32)
-    weights = jnp.zeros((MROWS, 64), F32)
+    for i in (5, 6, 7):
+        loads[i].wait()
+    ids = ids_ref[...]
+    raised = jnp.exp(logits_ref[...])
+    route = (raised / jnp.sum(raised, axis=0, keepdims=True)).astype(BF).astype(F32)
+    expert = iota((64, MROWS), 0)
+    chosen = jnp.zeros((64, MROWS), F32)
+    weights = jnp.zeros((64, MROWS), F32)
     for j in range(TOPK):
-        hit = ids[:, j : j + 1] == lanes
+        hit = ids[j : j + 1, :] == expert
         chosen = chosen + jnp.where(hit, 1.0, 0.0)
-        weights = weights + jnp.where(hit, route[:, j : j + 1], 0.0)
+        weights = weights + jnp.where(hit, route[j : j + 1, :], 0.0)
     r = iota((SLOTS, 64), 0)
     r_xc = (r >> 2) & 7
     r_slot = ((r_xc >> 1) * NZ + (r >> 5)) * 2 + (r_xc & 1)
     lands = jnp.where(home_ref[...] == r_slot, 1.0, 0.0).astype(BF)
-    chosen_r = dot(chosen.astype(BF), lands, 1, 1)
-    weights_r = dot(weights.astype(BF), lands, 1, 1)
+    chosen_r = dot(chosen.astype(BF), lands, 0, 1)
+    weights_r = dot(weights.astype(BF), lands, 0, 1)
     earlier = jnp.where(iota((MROWS, MROWS), 1) < iota((MROWS, MROWS), 0), 1.0, 0.0).astype(BF)
     rank = dot(earlier, chosen_r.astype(BF))
     right_rank = rank == (iota((MROWS, SLOTS), 1) & 3).astype(F32)
@@ -102,7 +110,8 @@
     pr, pc = iota((SLOTS, SLOTS), 0), iota((SLOTS, SLOTS), 1)
     perm_ref[...] = jnp.where(pc == ((pr >> 2) & 7) * 32 + (pr >> 5) * 4 + (pr & 3), 1.0, 0.0).astype(BF)
 
-    qall[c] = q_ref[0]
+    loads[4].wait()
+    loads[8].wait()
     pl.semaphore_wait(barrier, 29)
 
     def send(src, dst, s_sem, r_sem, ee, cc):
@@ -114,7 +123,7 @@
         pltpu.make_async_copy(ref, ref, sem).wait()
 
     for dy, dx in SEND_ORDER:
-        send(q_ref.at[0], qall.at[c], send_sem.at[0], q_sem, e, ctx_peer(dy, dx))
+        send(qall.at[c], qall.at[c], send_sem.at[0], q_sem, e, ctx_peer(dy, dx))
     loads[0].wait()
     await_bytes(qall.at[pl.ds(0, 15)], q_sem)
 
@@ -184,55 +193,74 @@
 
     raw = rows32 * (1.0 / gain)
     squares = jnp.sum(raw * raw, axis=1, keepdims=True)
+    rows_ref[...] = rows
     lane16 = iota((16, 128), 1)
-    tiles = []
     for rb in range(4):
-        a, b, cc = (squares[rb * RB + t * 16 : rb * RB + t * 16 + 16] for t in range(3))
-        tiles.append(jnp.where(lane16 < 32, a, jnp.where(lane16 < 64, b, cc)).astype(BF))
+        parts = [squares[rb * RB + t * 16 : rb * RB + t * 16 + 16] for t in range(3)]
+        tiles_ref[rb] = jnp.where(lane16 < 32, parts[0], jnp.where(lane16 < 64, parts[1], parts[2])).astype(BF)
     loads[2].wait()
-    my_cb = c // 4
-    for step in (2, 1, 3, 0):
-        cb = (my_cb + step) % 4
+    partner = y * 2 + 1 - xl
+
+    def merge(dy):
+        await_bytes(xr.at[dy], x_sem.at[dy])
+        both = own[dy].astype(F32) + xr[dy].astype(F32)
+        if dy == 0:
+            acc[...] = both
+        else:
+            ys[dy - 1] = both.astype(BF)
+            send(ys.at[dy - 1], yr.at[dy - 1], send_sem.at[6], y_sem.at[dy - 1], e, ctx_peer(dy, 0))
+
+    order = (4, 3, 5, 2, 6, 1, 7, 0)
+    for n, dy in enumerate(order):
+        to = (y + dy) % NY
+        low = (to % 2) * 2
+        block = [
+            rows_ref[pl.ds(pl.multiple_of((low + x) * RB, 16), RB), :] for x in (xl, 1 - xl)
+        ]
+        left = jnp.concatenate(block, axis=0)
         for half in range(2):
-            start = pl.multiple_of(half * FF + cb * CB, 128)
-            part = dot(rows, gu[:, pl.ds(start, CB)]).astype(BF)
-            for rb in range(4):
-                for t in range(3):
-                    at = (half * 3 + t) * RB
-                    es[cb * 4 + rb, at : at + RB, :] = part[rb * RB : rb * RB + RB, t * 128 : t * 128 + 128]
-        for rb in range(4):
-            es[cb * 4 + rb, 6 * RB : CHUNK, :] = tiles[rb]
-        for rb in range(4):
-            peer = cb * 4 + rb
-            slot = ((peer // 2 - y) % NY) * 2 + (peer + xl) % 2
-
-            @pl.when(peer != c)
-            def _():
-                send(es.at[peer], er.at[slot], send_sem.at[5], e_sem.at[slot], e, peer)
-
-    acc[...] = es[c].astype(F32)
-    for n, (dy, dx) in enumerate(SEND_ORDER):
-        j = dy * 2 + dx
-        await_bytes(er.at[j], e_sem.at[j])
-        acc[...] += er[j].astype(F32)
+            start = pl.multiple_of(half * FF + (to // 2) * CB, 128)
+            part = dot(left, gu[:, pl.ds(start, CB)]).astype(BF)
+            for t in range(3):
+                at = (half * 3 + t) * RB
+                own[dy, at : at + RB, :] = part[0:RB, t * 128 : t * 128 + 128]
+                xs[dy, at : at + RB, :] = part[RB : 2 * RB, t * 128 : t * 128 + 128]
+        own[dy, 6 * RB : CHUNK, :] = tiles_ref[low + xl]
+        xs[dy, 6 * RB : CHUNK, :] = tiles_ref[low + 1 - xl]
+        send(xs.at[dy], xr.at[dy], send_sem.at[5], x_sem.at[dy], e, partner)
+        if n >= 3:
+            merge(order[n - 3])
+    for dy in order[5:]:
+        merge(dy)
+    for dy in (1, 7, 2, 6, 3, 5, 4):
+        await_bytes(yr.at[dy - 1], y_sem.at[dy - 1])
+        acc[...] += yr[dy - 1].astype(F32)
     scale16 = lax.rsqrt(acc[6 * RB : CHUNK, :] * (1.0 / D) + 1e-06)
     scale = jnp.concatenate([scale16[:, 0:1], scale16[:, 32:33], scale16[:, 64:65]], axis=0)
     for t in range(3):
         gate = acc[t * RB : t * RB + RB, :] * scale
         upper = acc[(3 + t) * RB : (4 + t) * RB, :] * scale
         fs[:, t * 128 : t * 128 + 128] = (gate / (1.0 + jnp.exp(-gate)) * upper).astype(BF)
-    row_at = pl.multiple_of((c % 4) * RB, 16)
-    col_at = pl.multiple_of(my_cb * CB, 128)
-    mine = hid.at[pl.ds(row_at, RB), pl.ds(col_at, CB)]
-    for dy, dx in SEND_ORDER:
-        send(fs, mine, fsend_sem.at[dy * 2 + dx], f_sem.at[dy * 2 + dx], e, ctx_peer(dy, dx))
-    hid[pl.ds(row_at, RB), pl.ds(col_at, CB)] = fs[...]
+    def place(cc):
+        return hid.at[
+            pl.ds(pl.multiple_of((cc % 4) * RB, 16), RB), pl.ds(pl.multiple_of((cc // 4) * CB, 128), CB)
+        ]
+
+    near = (1, 7, 2, 6, 3, 5, 4)
+    send(fs, place(c), fsend_sem.at[0], fx_sem.at[0], e, partner)
+    for dy in near:
+        send(fs, place(c), fsend_sem.at[dy], fy_sem.at[dy], e, ctx_peer(dy, 0))
+    hid[pl.ds(pl.multiple_of((c % 4) * RB, 16), RB), pl.ds(pl.multiple_of((c // 4) * CB, 128), CB)] = fs[...]
     stretch = jnp.where(
         iota((SLOTS, ROWS), 0) == (iota((SLOTS, ROWS), 1) & 63) * 4 + (iota((SLOTS, ROWS), 1) >> 6), 1.0, 0.0
     ).astype(BF)
     loads[3].wait()
-    for dy, dx in SEND_ORDER:
-        await_bytes(fs, f_sem.at[dy * 2 + dx])
+    for dy in near:
+        source = place(ctx_peer(NY - dy, 0))
+        await_bytes(fs, fy_sem.at[dy])
+        send(source, source, fsend_sem.at[NY + dy], fx_sem.at[dy], e, partner)
+    for dy in (0,) + near:
+        await_bytes(fs, fx_sem.at[dy])
     result = dot(hid[...], dn[...]).astype(BF)
 
     g1s[...] = dot(stretch, result).astype(BF).reshape(NXC, 32, 256)
@@ -254,8 +282,11 @@
     await_bytes(cr.at[pl.ds(0, 15)], send_sem.at[2])
     await_bytes(d1r.at[pl.ds(0, 7)], send_sem.at[3])
     await_bytes(d2r.at[pl.ds(0, 7)], send_sem.at[4])
-    await_bytes(er.at[pl.ds(0, 15)], send_sem.at[5])
-    for j in range(1, CTX):
+    await_bytes(xr, send_sem.at[5])
+    await_bytes(yr, send_sem.at[6])
+    for j in range(8):
+        await_bytes(fs, fsend_sem.at[j])
+    for j in range(9, 16):
         await_bytes(fs, fsend_sem.at[j])
     await_bytes(g1r.at[pl.ds(0, 7)], send_sem.at[7])
     await_bytes(g2r.at[pl.ds(0, 7)], send_sem.at[8])
@@ -269,9 +300,13 @@
     return pl.pallas_call(
         kernel,
         out_shape=jax.ShapeDtypeStruct((1, MROWS, 256), BF),
-        in_specs=[vm, hb, hb, vm, vm, vm, vm, hb, hb],
+        in_specs=[hb] * 9,
         out_specs=vm,
         scratch_shapes=[
+            vmem((TOPK, MROWS), jnp.int32),
+            vmem((TOPK, MROWS), F32),
+            vmem((1, 64), jnp.int32),
+            vmem((1, 256), F32),
             vmem((128, 512), BF),
             vmem((256, D), BF),
             vmem((256, 2 * FF), BF),
@@ -285,8 +320,13 @@
             vmem((NZ, 32, 256), BF),
             vmem((NXC, 32, 256), BF),
             vmem((NXC, 32, 256), BF),
-            vmem((CTX, CHUNK, 128), BF),
-            vmem((CTX, CHUNK, 128), BF),
+            vmem((ROWS, 256), BF),
+            vmem((4, 16, 128), BF),
+            vmem((NY, CHUNK, 128), BF),
+            vmem((NY, CHUNK, 128), BF),
+            vmem((NY, CHUNK, 128), BF),
+            vmem((NY - 1, CHUNK, 128), BF),
+            vmem((NY - 1, CHUNK, 128), BF),
             vmem((CHUNK, 128), F32),
             vmem((RB, CB), BF),
             vmem((ROWS, FF), BF),
@@ -297,20 +337,22 @@
             vmem((MROWS, SLOTS), BF),
             vmem((MROWS, SLOTS), BF),
             vmem((SLOTS, SLOTS), BF),
-            dma((4,)),
+            dma((9,)),
             dma((9,)),
             dma, dma, dma, dma, dma,
-            dma((CTX,)),
-            dma((CTX,)),
-            dma((CTX,)),
+            dma((NY,)),
+            dma((NY - 1,)),
+            dma((2 * NY,)),
+            dma((NY,)),
+            dma((NY,)),
             dma, dma,
         ],
         compiler_params=pltpu.CompilerParams(
-            collective_id=0, has_side_effects=True, vmem_limit_bytes=40 * 1024 * 1024
+            collective_id=0, has_side_effects=True, vmem_limit_bytes=63 * 1024 * 1024
         ),
     )(
-        queries, keys_values, out_proj, norm_gain.reshape(1, 256), expert_ids, route_logits,
-        home.reshape(1, 64), gate_up, down,
+        queries, keys_values, out_proj, norm_gain.reshape(1, 256), jnp.swapaxes(expert_ids, 1, 2),
+        jnp.swapaxes(route_logits, 1, 2), home.reshape(1, 64), gate_up, down,
     )
 
 

time: 127 us -> 99.7 us (0.79)
  Pallas kernels: 118 us -> 98.1 us
  local copies, waits for them, and re-layouts: 9.18 us -> 1.3 us
    pallas_call x1, Pallas kernels: 118 us -> 98.1 us  [body(): pl.pallas_call(kernel, out_shape=jax.ShapeDtypeStruct((1, MROWS, 256), BF...]
    unnamed x17 -> x1, local copies, waits for them, and re-layouts: 9.18 us -> 1.3 us
where the time goes in v2:
time: 99.7 us; the launch traced here: 99.4 us
  Pallas kernels  98.1 us (98%)
  local copies, waits for them, and re-layouts  1.3 us (1%)
    pallas_call x1, Pallas kernels, body(): pl.pallas_call(kernel, out_shape=jax.ShapeDtypeStruct((1, MROWS, 256), BF...  98.1 us

profile of v2, /device:TPU:1, one launch (start us, length us, event | category | flops | bytes accessed | tf_op | source)
XLA Modules:
  0.0 99.4 jit_solution(11802271362585553326)
XLA Ops:
  0.0 98.1 %shard_map.91 = bf16[1,16,256]{2,1,0:T(8,128)(2,1)} custom-call(bf16[1,16,256]{2,1,0:T(8,128)(2,1)} %q_hbm.1, bf16[1,128,512]{2,1,0:T(8,128)(2,1)} %kv_hbm.1, bf16[256,4096]{1,0:T(8,128)(2,1)} %op_hbm.1, f32[1,256]{1,0:T(1,128)} %bitcast.6, s32[1,8,16]{2,1,0:T(8,128)} %bitcast.4, f32[1,8,16]{2,1,0:T(8,128)} %bitcast.5, s32[1,64]{1,0:T(1,128)} %bitcast.7, ...), custom_call_target="tpu_custom_call" | custom-call | tf_op jit(solution)/shard_map/pallas_call | solution.py:300
  98.1 1.3 %copy.11 = bf16[1,16,256]{2,1,0:T(8,128)(2,1)} copy(bf16[1,16,256]{2,1,0:T(8,128)(2,1)} %shard_map.91) | data formatting | bytes 16384

commit v3 on v2

v3 whole, which is shorter than its diff:
```python
import functools

import jax
import jax.numpy as jnp
from jax import lax
from jax.experimental import pallas as pl
from jax.experimental.pallas import tpu as pltpu
from jax.sharding import PartitionSpec as P

MESH = pl.DeviceIdType.MESH
BF = jnp.bfloat16
F32 = jnp.float32

D = 4096
FF = 1536
HD = 128
MROWS = 16
TOPK = 8
CTX = 16
NY = 8
NZ = 8
NX = 4
CHIPS = NX * NZ
SLOTS = 256
ROWS = 192
RB = 48
CB = 384
CHUNK = 6 * RB + 16
SEND_ORDER = [(dy, dx) for dy in (4, 3, 5, 2, 6, 1, 7, 0) for dx in (1, 0) if (dy, dx) != (0, 0)]

CHIP_ORDER = sorted(
    [(dx, dz) for dx in range(NX) for dz in range(NZ) if (dx, dz) != (0, 0)],
    key=lambda at: -(2 * min(at[0], NX - at[0]) + min(at[1], NZ - at[1])),
)


def iota(shape, dim):
    return lax.broadcasted_iota(jnp.int32, shape, dim)


def dot(a, b, ca=1, cb=0):
    return lax.dot_general(a, b, (((ca,), (cb,)), ((), ())), preferred_element_type=F32)


def kernel(
    q_hbm, kv_hbm, op_hbm, gain_hbm, ids_hbm, logits_hbm, home_hbm, gu_hbm, dn_hbm, out_ref,
    ids_ref, logits_ref, home_ref, gain_ref,
    kv, op, gu, dn, qall, nb, nr, cs, cr, rows2, ds, dr, rows_ref, tiles_ref, made, xr, ys, yr, yd, held, acc, fs, hid,
    gs, gr, half_s, half_r, tab, tab_s,
    load_sem, send_sem, q_sem, n_sem, c_sem, t_sem, s_sem, d_sem, esend_sem, x_sem, y_sem, fsend_sem, fy_sem, fx_sem, g_sem, h_sem, ring_sem,
):
    e = lax.axis_index("expert")
    c = lax.axis_index("context")
    y, xl = c // 2, c % 2
    core, z, xh = e % 2, (e // 2) % NZ, e // (2 * NZ)
    chip = e // 2
    sibling = chip * 2 + 1 - core
    sign = 1 - 2 * core

    loads = [
        pltpu.make_async_copy(src, dst, load_sem.at[i])
        for i, (src, dst) in enumerate(
            [
                (kv_hbm.at[0], kv), (op_hbm, op), (gu_hbm.at[0], gu), (dn_hbm.at[0], dn),
                (q_hbm.at[0], qall.at[c]), (ids_hbm.at[0], ids_ref), (logits_hbm.at[0], logits_ref),
                (home_hbm, home_ref), (gain_hbm, gain_ref),
            ]
        )
    ]
    for i in (5, 6, 7, 4, 8, 0, 1, 2, 3):
        loads[i].start()

    def ctx_peer(dy, dx):
        return ((y + dy) % NY) * 2 + (xl + dx) % 2

    def y_peer(k):
        return ((y + NY + sign * k) % NY) * 2 + xl

    def chip_peer(dx, dz):
        return ((xh + dx) % NX) * NZ + (z + dz) % NZ

    barrier = pltpu.get_barrier_semaphore()

    def greet(ee, cc):
        pl.semaphore_signal(barrier, inc=1, device_id=(ee, cc), device_id_type=MESH)

    for dy, dx in SEND_ORDER:
        greet(e, ctx_peer(dy, dx))
    for dz in (4, 3, 5, 2, 6, 1, 7):
        greet(chip_peer(0, dz) * 2 + core, c)
    for dx in (2, 1, 3):
        greet(chip_peer(dx, 0) * 2 + core, c)
    greet(sibling, c)
    loads[4].wait()
    pl.semaphore_wait(barrier, 26)

    def send(src, dst, s_sem, r_sem, ee, cc):
        pltpu.make_async_remote_copy(
            src_ref=src, dst_ref=dst, send_sem=s_sem, recv_sem=r_sem, device_id=(ee, cc), device_id_type=MESH
        ).start()

    def await_bytes(ref, sem):
        pltpu.make_async_copy(ref, ref, sem).wait()

    for dy, dx in SEND_ORDER:
        send(qall.at[c], qall.at[c], send_sem.at[0], q_sem, e, ctx_peer(dy, dx))
    for dx in (2, 1, 3):
        pl.semaphore_signal(ring_sem, inc=1, device_id=(chip_peer(dx, 0) * 2 + core, c), device_id_type=MESH)

    for i in (5, 6, 7):
        loads[i].wait()
    ids = ids_ref[...]
    raised = jnp.exp(logits_ref[...])
    route = (raised / jnp.sum(raised, axis=0, keepdims=True)).astype(BF).astype(F32)
    expert = iota((64, MROWS), 0)
    chosen = jnp.zeros((64, MROWS), F32)
    weights = jnp.zeros((64, MROWS), F32)
    for j in range(TOPK):
        hit = ids[j : j + 1, :] == expert
        chosen = chosen + jnp.where(hit, 1.0, 0.0)
        weights = weights + jnp.where(hit, route[j : j + 1, :], 0.0)
    chosen, weights = chosen.astype(BF), weights.astype(BF)
    earlier = jnp.where(iota((MROWS, MROWS), 1) < iota((MROWS, MROWS), 0), 1.0, 0.0).astype(BF)
    column = iota((MROWS, SLOTS), 1)
    wanted = jnp.where(((column >> 2) & 1) == core, column & 3, -1).astype(F32)
    for side in (1, 0):
        at_core = (core + side) % 2
        lands = jnp.where(home_ref[...] == (iota((SLOTS, 64), 0) >> 3) * 2 + at_core, 1.0, 0.0).astype(BF)
        chosen_r = dot(chosen, lands, 0, 1)
        weights_r = dot(weights, lands, 0, 1)
        right_rank = dot(earlier, chosen_r.astype(BF)) == wanted
        both = jnp.concatenate(
            [jnp.where(right_rank, chosen_r, 0.0), jnp.where(right_rank, weights_r, 0.0)], axis=0
        ).astype(BF)
        if side == 1:
            tab_s[...] = both
            send(tab_s, tab.at[core], send_sem.at[3], t_sem, sibling, c)
        else:
            tab[core] = both

    loads[0].wait()
    await_bytes(qall.at[pl.ds(0, 15)], q_sem)

    visible = (iota((128, 128), 0) & 15) >= c
    for g in range(2):
        key, value = kv[:, g * HD : (g + 1) * HD], kv[:, (2 + g) * HD : (3 + g) * HD]
        denoms = []
        for p in range(2):
            query = qall[8 * g : 8 * g + 8, :, p * HD : (p + 1) * HD].reshape(128, HD)
            scores = dot(query, key, 1, 1) * HD ** (-0.5)
            weight = jnp.where(visible, jnp.exp(scores), 0.0)
            denoms.append(jnp.sum(weight, axis=1, keepdims=True))
            numer = dot(weight.astype(BF), value)
            nb[8 * g : 8 * g + 8, :, p * HD : (p + 1) * HD] = numer.astype(BF).reshape(8, MROWS, HD)
        lane = iota((128, 128), 1)
        both = jnp.where(lane < 64, denoms[0], denoms[1])
        high = both.astype(BF).astype(F32)
        packed = jnp.where((lane & 63) < 32, high, both - high)
        nb[8 * g : 8 * g + 8, :, 256:384] = packed.astype(BF).reshape(8, MROWS, 128)

    for dy, dx in SEND_ORDER:
        peer = ctx_peer(dy, dx)
        send(nb.at[peer], nr.at[dy * 2 + dx], send_sem.at[1], n_sem, e, peer)
    nr[0] = nb[c]
    await_bytes(nr.at[pl.ds(1, 15)], n_sem)
    total = nr[0].astype(F32)
    for j in range(1, CTX):
        total = total + nr[j].astype(F32)
    denom0 = total[:, 256:257] + total[:, 288:289]
    denom1 = total[:, 320:321] + total[:, 352:353]
    attended = jnp.concatenate([total[:, 0:128] / denom0, total[:, 128:256] / denom1], axis=1).astype(BF)

    loads[1].wait()
    for dy, dx in SEND_ORDER + [(0, 0)]:
        peer = ctx_peer(dy, dx)
        j = dy * 2 + dx
        part = dot(attended, op[:, pl.ds(pl.multiple_of(peer * 256, 256), 256)]).astype(BF)
        if j == 0:
            cr[0] = part
        else:
            cs[j] = part
            send(cs.at[j], cr.at[j], send_sem.at[2], c_sem, e, peer)
    await_bytes(cr.at[pl.ds(1, 15)], c_sem)
    projected = cr[0].astype(F32)
    for j in range(1, CTX):
        projected = projected + cr[j].astype(F32)
    loads[8].wait()
    gain = gain_ref[...]
    rows2[core] = (projected * gain).astype(BF)

    send(rows2.at[core], rows2.at[core], send_sem.at[4], s_sem, sibling, c)
    squeeze = jnp.where(
        iota((ROWS, SLOTS), 1) == (iota((ROWS, SLOTS), 0) & 63) * 4 + (iota((ROWS, SLOTS), 0) >> 6), 1.0, 0.0
    ).astype(BF)
    await_bytes(tab_s, t_sem)
    picks = tab[:, 0:MROWS, :].reshape(2 * MROWS, SLOTS)
    await_bytes(rows2.at[0], s_sem)
    slot_rows = dot(picks, rows2[...].reshape(2 * MROWS, 256), 0, 0).astype(BF)
    ds[:, 0:8, :] = slot_rows[:, 0:128].reshape(CHIPS, 8, 128)
    ds[:, 8:16, :] = slot_rows[:, 128:256].reshape(CHIPS, 8, 128)
    pl.semaphore_wait(ring_sem, NX - 1)
    for dx, dz in CHIP_ORDER:
        peer = chip_peer(dx, dz)
        send(ds.at[peer], dr.at[chip], send_sem.at[7], d_sem, peer * 2 + core, c)
    dr[chip] = ds[chip]
    await_bytes(dr.at[pl.ds(0, CHIPS - 1)], d_sem)
    arrived = jnp.concatenate(
        [dr[:, 0:8, :].reshape(SLOTS, 128), dr[:, 8:16, :].reshape(SLOTS, 128)], axis=1
    )
    rows32 = dot(squeeze, arrived)
    rows = rows32.astype(BF)

    raw = rows32 * (1.0 / gain)
    squares = jnp.sum(raw * raw, axis=1, keepdims=True)
    rows_ref[...] = rows
    lane16 = iota((16, 128), 1)
    for rb in range(4):
        parts = [squares[rb * RB + t * 16 : rb * RB + t * 16 + 16] for t in range(3)]
        tiles_ref[rb] = jnp.where(lane16 < 32, parts[0], jnp.where(lane16 < 64, parts[1], parts[2])).astype(BF)
    loads[2].wait()
    partner = y * 2 + 1 - xl

    def make(k):
        to = (y + NY + sign * k) % NY
        low = (to % 2) * 2
        block = [rows_ref[pl.ds(pl.multiple_of((low + x) * RB, 16), RB), :] for x in (xl, 1 - xl)]
        left = jnp.concatenate(block, axis=0)
        for half in range(2):
            start = pl.multiple_of(half * FF + (to // 2) * CB, 128)
            part = dot(left, gu[:, pl.ds(start, CB)]).astype(BF)
            for t in range(3):
                at = (half * 3 + t) * RB
                for side in range(2):
                    made[k, side, at : at + RB, :] = part[side * RB : side * RB + RB, t * 128 : t * 128 + 128]
        made[k, 0, 6 * RB : CHUNK, :] = tiles_ref[low + xl]
        made[k, 1, 6 * RB : CHUNK, :] = tiles_ref[low + 1 - xl]

    def send_x(src, n):
        send(src, xr.at[n], esend_sem.at[n], x_sem.at[n], e, partner)

    def take_x(n):
        await_bytes(xr.at[n], x_sem.at[n])
        return xr[n].astype(F32)

    def send_y(n, value, k):
        ys[n] = value.astype(BF)
        send(ys.at[n], yr.at[n], esend_sem.at[6 + n], y_sem.at[n], e, y_peer(k))

    def take_y(n):
        await_bytes(yr.at[n], y_sem.at[n])
        return yr[n].astype(F32)

    def send_pair(n, k, steps):
        send(made.at[k], yd.at[n], esend_sem.at[11 + n], y_sem.at[5 + n], e, y_peer(steps))

    def mine(k):
        return made[k, 0].astype(F32)

    make(4)
    send_x(made.at[4, 1], 0)
    make(3)
    send_x(made.at[3, 1], 1)
    make(5)
    send_x(made.at[5, 1], 2)
    make(1)
    send_pair(0, 1, 1)
    make(2)
    send_x(made.at[2, 1], 3)
    make(7)
    send_pair(1, 7, -1)
    make(6)
    send_x(made.at[6, 1], 4)
    send_y(0, mine(4) + take_x(0), 2)
    make(0)
    send_y(1, mine(3) + take_x(1), 1)
    send_y(2, mine(5) + take_x(2), -1)
    for n in range(2):
        await_bytes(yd.at[n], y_sem.at[5 + n])
    held[...] = (made[0, 1].astype(F32) + yd[0, 1].astype(F32) + yd[1, 1].astype(F32)).astype(BF)
    send_x(held, 5)
    acc[...] = mine(0) + yd[0, 0].astype(F32) + yd[1, 0].astype(F32)
    send_y(3, mine(2) + take_x(3) + take_y(0) + take_y(1), 2)
    send_y(4, mine(6) + take_x(4) + take_y(2), -2)
    acc[...] += take_x(5)
    acc[...] += take_y(3) + take_y(4)
    scale16 = lax.rsqrt(acc[6 * RB : CHUNK, :] * (1.0 / D) + 1e-06)
    scale = jnp.concatenate([scale16[:, 0:1], scale16[:, 32:33], scale16[:, 64:65]], axis=0)
    for t in range(3):
        gate = acc[t * RB : t * RB + RB, :] * scale
        upper = acc[(3 + t) * RB : (4 + t) * RB, :] * scale
        fs[:, t * 128 : t * 128 + 128] = (gate / (1.0 + jnp.exp(-gate)) * upper).astype(BF)
    def place(cc):
        return hid.at[
            pl.ds(pl.multiple_of((cc % 4) * RB, 16), RB), pl.ds(pl.multiple_of((cc // 4) * CB, 128), CB)
        ]

    def there(k):
        return place(y_peer(k))

    def across(k):
        return place(y_peer(k) + 1 - 2 * xl)

    def pass_on(n, src, dst, sems, k, peer):
        send(src, dst, fsend_sem.at[n], sems.at[k + 3], e, peer)

    pass_on(0, fs, place(c), fx_sem, 0, partner)
    pass_on(1, fs, place(c), fy_sem, -2, y_peer(2))
    pass_on(2, fs, place(c), fy_sem, 2, y_peer(-2))
    pass_on(3, fs, place(c), fy_sem, -1, y_peer(1))
    pass_on(4, fs, place(c), fy_sem, 1, y_peer(-1))
    hid[pl.ds(pl.multiple_of((c % 4) * RB, 16), RB), pl.ds(pl.multiple_of((c // 4) * CB, 128), CB)] = fs[...]
    stretch = jnp.where(
        iota((SLOTS, ROWS), 0) == (iota((SLOTS, ROWS), 1) & 63) * 4 + (iota((SLOTS, ROWS), 1) >> 6), 1.0, 0.0
    ).astype(BF)
    loads[3].wait()
    await_bytes(fs, fx_sem.at[3])
    pass_on(5, across(0), across(0), fx_sem, -1, y_peer(1))
    pass_on(6, across(0), across(0), fx_sem, 1, y_peer(-1))
    await_bytes(fs, fy_sem.at[1])
    pass_on(7, there(-2), there(-2), fy_sem, 4, y_peer(2))
    pass_on(8, there(-2), there(-2), fy_sem, -3, y_peer(1))
    pass_on(9, there(-2), there(-2), fx_sem, -2, partner)
    await_bytes(fs, fy_sem.at[5])
    pass_on(10, there(2), there(2), fy_sem, 3, y_peer(-1))
    pass_on(11, there(2), there(2), fx_sem, 2, partner)
    for n, k in ((12, -3), (13, 3), (14, 4)):
        await_bytes(fs, fy_sem.at[k + 3])
        pass_on(n, there(k), there(k), fx_sem, k, partner)
    for k in (-1, 1):
        await_bytes(fs, fy_sem.at[k + 3])
    for k in (-1, 1, -2, 2, -3, 3, 4):
        await_bytes(fs, fx_sem.at[k + 3])
    result = dot(hid[...], dn[...]).astype(BF)

    back = dot(stretch, result).astype(BF)
    gs[:, 0:8, :] = back[:, 0:128].reshape(CHIPS, 8, 128)
    gs[:, 8:16, :] = back[:, 128:256].reshape(CHIPS, 8, 128)
    for dx, dz in CHIP_ORDER:
        peer = chip_peer(dx, dz)
        send(gs.at[peer], gr.at[chip], send_sem.at[8], g_sem, peer * 2 + core, c)
    gr[chip] = gs[chip]
    combine = tab[:, MROWS : 2 * MROWS, :].reshape(2 * MROWS, SLOTS)
    await_bytes(gr.at[pl.ds(0, CHIPS - 1)], g_sem)
    returned = jnp.concatenate(
        [gr[:, 0:8, :].reshape(SLOTS, 128), gr[:, 8:16, :].reshape(SLOTS, 128)], axis=1
    )
    half_s[...] = dot(combine, returned).reshape(2, MROWS, 256)
    send(half_s.at[1 - core], half_r, send_sem.at[9], h_sem, sibling, c)
    await_bytes(half_r, h_sem)
    out_ref[0] = (half_s[core] + half_r[...]).astype(BF)

    await_bytes(qall.at[pl.ds(0, 15)], send_sem.at[0])
    await_bytes(nr.at[pl.ds(0, 15)], send_sem.at[1])
    await_bytes(cr.at[pl.ds(0, 15)], send_sem.at[2])
    await_bytes(tab_s, send_sem.at[3])
    await_bytes(rows2.at[0], send_sem.at[4])
    for n in range(11):
        await_bytes(held, esend_sem.at[n])
    for n in range(2):
        await_bytes(yd.at[n], esend_sem.at[11 + n])
    for n in range(15):
        await_bytes(fs, fsend_sem.at[n])
    await_bytes(dr.at[pl.ds(0, CHIPS - 1)], send_sem.at[7])
    await_bytes(gr.at[pl.ds(0, CHIPS - 1)], send_sem.at[8])
    await_bytes(half_r, send_sem.at[9])


def body(queries, keys_values, out_proj, norm_gain, expert_ids, route_logits, home, gate_up, down):
    vm = pl.BlockSpec(memory_space=pltpu.VMEM)
    hb = pl.BlockSpec(memory_space=pl.ANY)
    dma = pltpu.SemaphoreType.DMA
    vmem = pltpu.VMEM
    return pl.pallas_call(
        kernel,
        out_shape=jax.ShapeDtypeStruct((1, MROWS, 256), BF),
        in_specs=[hb] * 9,
        out_specs=vm,
        scratch_shapes=[
            vmem((TOPK, MROWS), jnp.int32),
            vmem((TOPK, MROWS), F32),
            vmem((1, 64), jnp.int32),
            vmem((1, 256), F32),
            vmem((128, 512), BF),
            vmem((256, D), BF),
            vmem((256, 2 * FF), BF),
            vmem((FF, 256), BF),
            vmem((CTX, MROWS, 256), BF),
            vmem((CTX, MROWS, 384), BF),
            vmem((CTX, MROWS, 384), BF),
            vmem((CTX, MROWS, 256), BF),
            vmem((CTX, MROWS, 256), BF),
            vmem((2, MROWS, 256), BF),
            vmem((CHIPS, 16, 128), BF),
            vmem((CHIPS, 16, 128), BF),
            vmem((ROWS, 256), BF),
            vmem((4, 16, 128), BF),
            vmem((NY, 2, CHUNK, 128), BF),
            vmem((6, CHUNK, 128), BF),
            vmem((5, CHUNK, 128), BF),
            vmem((5, CHUNK, 128), BF),
            vmem((2, 2, CHUNK, 128), BF),
            vmem((CHUNK, 128), BF),
            vmem((CHUNK, 128), F32),
            vmem((RB, CB), BF),
            vmem((ROWS, FF), BF),
            vmem((CHIPS, 16, 128), BF),
            vmem((CHIPS, 16, 128), BF),
            vmem((2, MROWS, 256), F32),
            vmem((MROWS, 256), F32),
            vmem((2, 2 * MROWS, SLOTS), BF),
            vmem((2 * MROWS, SLOTS), BF),
            dma((9,)),
            dma((10,)),
            dma, dma, dma, dma, dma, dma,
            dma((13,)),
            dma((6,)),
            dma((7,)),
            dma((15,)),
            dma((NY,)),
            dma((NY,)),
            dma, dma,
            pltpu.SemaphoreType.REGULAR,
        ],
        compiler_params=pltpu.CompilerParams(
            collective_id=0, has_side_effects=True, vmem_limit_bytes=63 * 1024 * 1024
        ),
    )(
        queries, keys_values, out_proj, norm_gain.reshape(1, 256), jnp.swapaxes(expert_ids, 1, 2),
        jnp.swapaxes(route_logits, 1, 2), home.reshape(1, 64), gate_up, down,
    )


def solution(mesh):
    in_specs = (
        P("expert", None, "context"),
        P("expert", "context", None),
        P("context", None),
        P("context"),
        P("expert", None, None),
        P("expert", None, None),
        P(),
        P("expert", "context", None),
        P("expert", None, "context"),
    )
    out_specs = P("expert", None, "context")
    return jax.shard_map(body, mesh=mesh, in_specs=in_specs, out_specs=out_specs, check_vma=False)
```

time: 99.7 us -> 90.8 us (0.911)
  Pallas kernels: 98.1 us -> 89.3 us
    pallas_call x1, Pallas kernels: 98.1 us -> 89.3 us  [body(): pl.pallas_call(kernel, out_shape=jax.ShapeDtypeStruct((1, MROWS, 256), BF...]
where the time goes in v3:
time: 90.8 us; the launch traced here: 90.6 us
  Pallas kernels  89.3 us (98%)
  local copies, waits for them, and re-layouts  1.3 us (1%)
    pallas_call x1, Pallas kernels, body(): pl.pallas_call(kernel, out_shape=jax.ShapeDtypeStruct((1, MROWS, 256), BF...  89.3 us

profile of v3, /device:TPU:1, one launch (start us, length us, event | category | flops | bytes accessed | tf_op | source)
XLA Modules:
  0.0 90.6 jit_solution(1851906315919648027)
XLA Ops:
  0.0 89.3 %shard_map.91 = bf16[1,16,256]{2,1,0:T(8,128)(2,1)} custom-call(bf16[1,16,256]{2,1,0:T(8,128)(2,1)} %q_hbm.1, bf16[1,128,512]{2,1,0:T(8,128)(2,1)} %kv_hbm.1, bf16[256,4096]{1,0:T(8,128)(2,1)} %op_hbm.1, f32[1,256]{1,0:T(1,128)} %bitcast.6, s32[1,8,16]{2,1,0:T(8,128)} %bitcast.4, f32[1,8,16]{2,1,0:T(8,128)} %bitcast.5, s32[1,64]{1,0:T(1,128)} %bitcast.7, ...), custom_call_target="tpu_custom_call" | custom-call | tf_op jit(solution)/shard_map/pallas_call | solution.py:373
  89.3 1.3 %copy.11 = bf16[1,16,256]{2,1,0:T(8,128)(2,1)} copy(bf16[1,16,256]{2,1,0:T(8,128)(2,1)} %shard_map.91) | data formatting | bytes 16384

commit v4 on v3

--- a/solution.py
+++ b/solution.py
@@ -142,26 +142,30 @@
     await_bytes(qall.at[pl.ds(0, 15)], q_sem)
 
     visible = (iota((128, 128), 0) & 15) >= c
-    for g in range(2):
-        key, value = kv[:, g * HD : (g + 1) * HD], kv[:, (2 + g) * HD : (3 + g) * HD]
+    lane = iota((128, 128), 1)
+    for far in (1, 0):
+        g = (y // 4 + far) % 2
+        key = kv[:, pl.ds(pl.multiple_of(g * HD, HD), HD)]
+        value = kv[:, pl.ds(pl.multiple_of((2 + g) * HD, HD), HD)]
+        heads = pl.ds(pl.multiple_of(8 * g, 8), 8)
         denoms = []
         for p in range(2):
-            query = qall[8 * g : 8 * g + 8, :, p * HD : (p + 1) * HD].reshape(128, HD)
+            query = qall[heads, :, p * HD : (p + 1) * HD].reshape(128, HD)
             scores = dot(query, key, 1, 1) * HD ** (-0.5)
             weight = jnp.where(visible, jnp.exp(scores), 0.0)
             denoms.append(jnp.sum(weight, axis=1, keepdims=True))
             numer = dot(weight.astype(BF), value)
-            nb[8 * g : 8 * g + 8, :, p * HD : (p + 1) * HD] = numer.astype(BF).reshape(8, MROWS, HD)
-        lane = iota((128, 128), 1)
+            nb[heads, :, p * HD : (p + 1) * HD] = numer.astype(BF).reshape(8, MROWS, HD)
         both = jnp.where(lane < 64, denoms[0], denoms[1])
         high = both.astype(BF).astype(F32)
         packed = jnp.where((lane & 63) < 32, high, both - high)
-        nb[8 * g : 8 * g + 8, :, 256:384] = packed.astype(BF).reshape(8, MROWS, 128)
-
-    for dy, dx in SEND_ORDER:
-        peer = ctx_peer(dy, dx)
-        send(nb.at[peer], nr.at[dy * 2 + dx], send_sem.at[1], n_sem, e, peer)
-    nr[0] = nb[c]
+        nb[heads, :, 256:384] = packed.astype(BF).reshape(8, MROWS, 128)
+        for step in (0, 3, 1, 2) if far else (2, 1, 3, 0):
+            for dx in (1, 0):
+                if far or (step, dx) != (0, 0):
+                    peer = (4 * g + (y + step) % 4) * 2 + (xl + dx) % 2
+                    send(nb.at[peer], nr.at[c], send_sem.at[1], n_sem, e, peer)
+    nr[c] = nb[c]
     await_bytes(nr.at[pl.ds(1, 15)], n_sem)
     total = nr[0].astype(F32)
     for j in range(1, CTX):

time: 90.8 us -> 89.9 us (0.990)
  no operation moved by 1% of the time
where the time goes in v4:
time: 89.9 us; the launch traced here: 89.7 us
  Pallas kernels  88.4 us (98%)
  local copies, waits for them, and re-layouts  1.3 us (1%)
    pallas_call x1, Pallas kernels, body(): pl.pallas_call(kernel, out_shape=jax.ShapeDtypeStruct((1, MROWS, 256), BF...  88.4 us

profile of v4, /device:TPU:1, one launch (start us, length us, event | category | flops | bytes accessed | tf_op | source)
XLA Modules:
  0.0 89.7 jit_solution(13898932863390423136)
XLA Ops:
  0.0 88.4 %shard_map.91 = bf16[1,16,256]{2,1,0:T(8,128)(2,1)} custom-call(bf16[1,16,256]{2,1,0:T(8,128)(2,1)} %q_hbm.1, bf16[1,128,512]{2,1,0:T(8,128)(2,1)} %kv_hbm.1, bf16[256,4096]{1,0:T(8,128)(2,1)} %op_hbm.1, f32[1,256]{1,0:T(1,128)} %bitcast.6, s32[1,8,16]{2,1,0:T(8,128)} %bitcast.4, f32[1,8,16]{2,1,0:T(8,128)} %bitcast.5, s32[1,64]{1,0:T(1,128)} %bitcast.7, ...), custom_call_target="tpu_custom_call" | custom-call | tf_op jit(solution)/shard_map/pallas_call | solution.py:377
  88.4 1.3 %copy.11 = bf16[1,16,256]{2,1,0:T(8,128)(2,1)} copy(bf16[1,16,256]{2,1,0:T(8,128)(2,1)} %shard_map.91) | data formatting | bytes 16384

commit v5 on v4

--- a/solution.py
+++ b/solution.py
@@ -26,6 +26,7 @@
 RB = 48
 CB = 384
 CHUNK = 6 * RB + 16
+PARTS = ((0, 3 * RB), (3 * RB, 3 * RB + 16))
 SEND_ORDER = [(dy, dx) for dy in (4, 3, 5, 2, 6, 1, 7, 0) for dx in (1, 0) if (dy, dx) != (0, 0)]
 
 CHIP_ORDER = sorted(
@@ -239,54 +240,66 @@
         made[k, 0, 6 * RB : CHUNK, :] = tiles_ref[low + xl]
         made[k, 1, 6 * RB : CHUNK, :] = tiles_ref[low + 1 - xl]
 
-    def send_x(src, n):
-        send(src, xr.at[n], esend_sem.at[n], x_sem.at[n], e, partner)
-
-    def take_x(n):
-        await_bytes(xr.at[n], x_sem.at[n])
-        return xr[n].astype(F32)
-
-    def send_y(n, value, k):
-        ys[n] = value.astype(BF)
-        send(ys.at[n], yr.at[n], esend_sem.at[6 + n], y_sem.at[n], e, y_peer(k))
-
-    def take_y(n):
-        await_bytes(yr.at[n], y_sem.at[n])
-        return yr[n].astype(F32)
+    def send_x(src, n, p):
+        at = pl.ds(*PARTS[p])
+        send(src.at[at], xr.at[n, at], esend_sem.at[2 * n + p], x_sem.at[2 * n + p], e, partner)
+
+    def take_x(n, p):
+        at = pl.ds(*PARTS[p])
+        await_bytes(xr.at[n, at], x_sem.at[2 * n + p])
+        return xr[n, at].astype(F32)
+
+    def send_y(n, p, value, k):
+        at = pl.ds(*PARTS[p])
+        ys[n, at] = value.astype(BF)
+        send(ys.at[n, at], yr.at[n, at], esend_sem.at[12 + 2 * n + p], y_sem.at[2 * n + p], e, y_peer(k))
+
+    def take_y(n, p):
+        at = pl.ds(*PARTS[p])
+        await_bytes(yr.at[n, at], y_sem.at[2 * n + p])
+        return yr[n, at].astype(F32)
 
     def send_pair(n, k, steps):
-        send(made.at[k], yd.at[n], esend_sem.at[11 + n], y_sem.at[5 + n], e, y_peer(steps))
-
-    def mine(k):
-        return made[k, 0].astype(F32)
-
-    make(4)
-    send_x(made.at[4, 1], 0)
-    make(3)
-    send_x(made.at[3, 1], 1)
-    make(5)
-    send_x(made.at[5, 1], 2)
+        send(made.at[k], yd.at[n], esend_sem.at[22 + n], y_sem.at[10 + n], e, y_peer(steps))
+
+    def mine(k, p):
+        return made[k, 0, pl.ds(*PARTS[p])].astype(F32)
+
+    def make_x(k, n):
+        make(k)
+        for p in range(2):
+            send_x(made.at[k, 1], n, p)
+
+    make_x(4, 0)
+    make_x(3, 1)
+    make_x(5, 2)
     make(1)
     send_pair(0, 1, 1)
-    make(2)
-    send_x(made.at[2, 1], 3)
+    make_x(2, 3)
     make(7)
     send_pair(1, 7, -1)
-    make(6)
-    send_x(made.at[6, 1], 4)
-    send_y(0, mine(4) + take_x(0), 2)
+    make_x(6, 4)
+    for p in range(2):
+        send_y(0, p, mine(4, p) + take_x(0, p), 2)
     make(0)
-    send_y(1, mine(3) + take_x(1), 1)
-    send_y(2, mine(5) + take_x(2), -1)
+    for p in range(2):
+        send_y(1, p, mine(3, p) + take_x(1, p), 1)
+    for p in range(2):
+        send_y(2, p, mine(5, p) + take_x(2, p), -1)
     for n in range(2):
-        await_bytes(yd.at[n], y_sem.at[5 + n])
+        await_bytes(yd.at[n], y_sem.at[10 + n])
     held[...] = (made[0, 1].astype(F32) + yd[0, 1].astype(F32) + yd[1, 1].astype(F32)).astype(BF)
-    send_x(held, 5)
-    acc[...] = mine(0) + yd[0, 0].astype(F32) + yd[1, 0].astype(F32)
-    send_y(3, mine(2) + take_x(3) + take_y(0) + take_y(1), 2)
-    send_y(4, mine(6) + take_x(4) + take_y(2), -2)
-    acc[...] += take_x(5)
-    acc[...] += take_y(3) + take_y(4)
+    for p in range(2):
+        send_x(held, 5, p)
+    acc[...] = made[0, 0].astype(F32) + yd[0, 0].astype(F32) + yd[1, 0].astype(F32)
+    for p in range(2):
+        send_y(3, p, mine(2, p) + take_x(3, p) + take_y(0, p) + take_y(1, p), 2)
+    for p in range(2):
+        send_y(4, p, mine(6, p) + take_x(4, p) + take_y(2, p), -2)
+    for p in range(2):
+        acc[pl.ds(*PARTS[p])] += take_x(5, p)
+    for p in range(2):
+        acc[pl.ds(*PARTS[p])] += take_y(3, p) + take_y(4, p)
     scale16 = lax.rsqrt(acc[6 * RB : CHUNK, :] * (1.0 / D) + 1e-06)
     scale = jnp.concatenate([scale16[:, 0:1], scale16[:, 32:33], scale16[:, 64:65]], axis=0)
     for t in range(3):
@@ -359,9 +372,10 @@
     await_bytes(tab_s, send_sem.at[3])
     await_bytes(rows2.at[0], send_sem.at[4])
     for n in range(11):
-        await_bytes(held, esend_sem.at[n])
+        for p in range(2):
+            await_bytes(held.at[pl.ds(*PARTS[p])], esend_sem.at[2 * n + p])
     for n in range(2):
-        await_bytes(yd.at[n], esend_sem.at[11 + n])
+        await_bytes(yd.at[n], esend_sem.at[22 + n])
     for n in range(15):
         await_bytes(fs, fsend_sem.at[n])
     await_bytes(dr.at[pl.ds(0, CHIPS - 1)], send_sem.at[7])
@@ -416,9 +430,9 @@
             dma((9,)),
             dma((10,)),
             dma, dma, dma, dma, dma, dma,
-            dma((13,)),
-            dma((6,)),
-            dma((7,)),
+            dma((24,)),
+            dma((12,)),
+            dma((12,)),
             dma((15,)),
             dma((NY,)),
             dma((NY,)),

time: 89.9 us -> 89.9 us (level)
  no operation moved by 1% of the time
where the time goes in v5:
time: 89.9 us; the launch traced here: 89.7 us
  Pallas kernels  88.4 us (98%)
  local copies, waits for them, and re-layouts  1.3 us (1%)
    pallas_call x1, Pallas kernels, body(): pl.pallas_call(kernel, out_shape=jax.ShapeDtypeStruct((1, MROWS, 256), BF...  88.4 us

profile of v5, /device:TPU:1, one launch (start us, length us, event | category | flops | bytes accessed | tf_op | source)
XLA Modules:
  0.0 89.7 jit_solution(7978380484934851576)
XLA Ops:
  0.0 88.4 %shard_map.91 = bf16[1,16,256]{2,1,0:T(8,128)(2,1)} custom-call(bf16[1,16,256]{2,1,0:T(8,128)(2,1)} %q_hbm.1, bf16[1,128,512]{2,1,0:T(8,128)(2,1)} %kv_hbm.1, bf16[256,4096]{1,0:T(8,128)(2,1)} %op_hbm.1, f32[1,256]{1,0:T(1,128)} %bitcast.6, s32[1,8,16]{2,1,0:T(8,128)} %bitcast.4, f32[1,8,16]{2,1,0:T(8,128)} %bitcast.5, s32[1,64]{1,0:T(1,128)} %bitcast.7, ...), custom_call_target="tpu_custom_call" | custom-call | tf_op jit(solution)/shard_map/pallas_call | solution.py:391
  88.4 1.3 %copy.11 = bf16[1,16,256]{2,1,0:T(8,128)(2,1)} copy(bf16[1,16,256]{2,1,0:T(8,128)(2,1)} %shard_map.91) | data formatting | bytes 16384
